TPU v7x, 512 devices: a whole 4x4x16 slice. The times are simulated.
512 devices in a mesh: row: 8 (over x_hi, y), col: 32 (over x_lo, z), head: 2 (over core).
Axes of the slice: x: 4 (x_hi: 2, x_lo: 2; x = x_hi * 2 + x_lo), y: 4, z: 16, core: 2. Of those that a mesh axis runs over, the one named last changes fastest.
Arguments:
- pair: bfloat16 [32, 4096, 128], P('row', 'col'), may hold values from -6 to 6
- layer_norm_gain: float32 [128], replicated, may hold values from 0.1 to 1.9
- w_proj: bfloat16 [128, 512], P(None, 'head'), may hold values from -0.5 to 0.5
- w_out: bfloat16 [128, 128], P('head'), may hold values from -0.5 to 0.5
- tri_bias: bfloat16 [4, 4096, 4096], P('head', 'col', 'row'), may hold values from -6 to 300
- active: int32 [16, 16], replicated, may hold values from 0 to 1, as said below
- d_out: bfloat16 [32, 4096, 128], P('row', 'col'), may hold values from -6 to 6
Outputs:
- out: bfloat16 [32, 4096, 128], P('row', 'col', 'head')
- pair_gradient: bfloat16 [32, 4096, 128], P('row', 'col')
Inputs may be any that keep to these rules, and one draw needn't show every extreme that they name: Entry [a, b] is 1 where key tile b is computed for query tile a; the table is symmetric and every tile is active with itself.
All inputs are finite; a program needn't handle non-finite values.
Results may differ from a plain program's by a relative error of at most 0.02.
Values may be sent and summed in bfloat16 or wider, within the bound.
No kernel may reach another device: no remote copies, remote signals or barrier semaphores. Data moves between devices by JAX's collectives and lax.ppermute only.
A program may use at most 64 MiB of HBM per device.

v0:
```python
import math
import jax
import jax.numpy as jnp
from jax import lax
from jax.sharding import PartitionSpec as P

DH = 32
TILE = 256
EPS = 1e-05
NEG = -1e30


def tile_onehot(first, count, tiles_total):
    index = (first + jnp.arange(count, dtype=jnp.int32)) // TILE
    return (index[:, None] == jnp.arange(tiles_total, dtype=jnp.int32)[None, :]).astype(jnp.float32)


def per_device(pair, layer_norm_gain, w_proj, w_out, tri_bias, active, d_out):
    rows, cols, width = pair.shape
    heads = w_out.shape[0] // DH
    scale = DH ** (-0.5)
    tiles_total = active.shape[0]
    x = pair.astype(jnp.float32)
    channel_average = jnp.mean(x, axis=-1, keepdims=True)
    centered_input = x - channel_average
    inverse_deviation = lax.rsqrt(
        jnp.mean(centered_input * centered_input, axis=-1, keepdims=True) + EPS
    )
    standardized_input = centered_input * inverse_deviation
    normalized_pair = (standardized_input * layer_norm_gain).astype(jnp.bfloat16)
    proj = jnp.einsum("rjc,cf->rjf", normalized_pair, w_proj, preferred_element_type=jnp.float32)
    proj = proj.reshape(rows, cols, heads, 4, DH)
    query = (proj[:, :, :, 0] * scale).astype(jnp.bfloat16)
    kv_local = proj[:, :, :, 1:3].astype(jnp.bfloat16).reshape(rows, cols, heads * 2 * DH)
    gate = jax.nn.sigmoid(proj[:, :, :, 3])
    col_start = lax.axis_index("col") * cols
    row_active = jnp.dot(tile_onehot(col_start, cols, tiles_total), active.astype(jnp.float32))
    gathered = lax.all_gather(kv_local, "col", axis=1, tiled=True)

    def block_parts(keys_values, piece, offset, first, step):
        bias_blk = lax.dynamic_slice_in_dim(piece, offset, step, 2)
        kv_blk = lax.dynamic_slice_in_dim(keys_values, first, step, 1).reshape(
            rows, step, heads, 2, DH
        )
        mask = jnp.dot(row_active, tile_onehot(first, step, tiles_total).T) > 0.5
        return (bias_blk, kv_blk[:, :, :, 0], kv_blk[:, :, :, 1], mask)

    def scores(key_blk, bias_blk, mask):
        score = jnp.einsum("rjhd,rkhd->rhjk", query, key_blk, preferred_element_type=jnp.float32)
        score = score + bias_blk[None].astype(jnp.float32)
        return jnp.where(mask[None, None], score, NEG)

    start_state = (
        jnp.full((rows, heads, cols), NEG, jnp.float32),
        jnp.zeros((rows, heads, cols), jnp.float32),
        jnp.zeros((rows, heads, cols, DH), jnp.float32),
    )
    piece = lax.all_gather(tri_bias, "row", axis=2, tiled=True)
    length = piece.shape[2]
    step = math.gcd(length, 2 * TILE)

    def forward_one_block(number, inner):
        offset = number * step
        bias_blk, key_blk, value_blk, mask = block_parts(gathered, piece, offset, offset, step)

        def forward_update(carry):
            run_max, run_sum, acc = carry
            score = scores(key_blk, bias_blk, mask)
            new_max = jnp.maximum(run_max, jnp.max(score, axis=-1))
            weights = jnp.where(mask[None, None], jnp.exp(score - new_max[..., None]), 0.0)
            factor = jnp.exp(run_max - new_max)
            run_sum = run_sum * factor + jnp.sum(weights, axis=-1)
            acc = acc * factor[..., None] + jnp.einsum(
                "rhjk,rkhd->rhjd",
                weights.astype(jnp.bfloat16),
                value_blk,
                preferred_element_type=jnp.float32,
            )
            return (new_max, run_sum, acc)

        return lax.cond(jnp.any(mask), forward_update, lambda carry: carry, inner)

    run_max, run_sum, acc = lax.fori_loop(0, length // step, forward_one_block, start_state)
    lse = run_max + jnp.log(run_sum)
    attended = jnp.transpose(acc / run_sum[..., None], (0, 2, 1, 3))
    gated = (gate * attended).astype(jnp.bfloat16).reshape(rows, cols, heads * DH)
    partial_out = jnp.einsum("rjf,fc->rjc", gated, w_out, preferred_element_type=jnp.float32)
    out = lax.psum_scatter(
        partial_out.astype(jnp.bfloat16), "head", scatter_dimension=2, tiled=True
    )
    d_go = jnp.einsum("rjc,fc->rjf", d_out, w_out, preferred_element_type=jnp.float32).reshape(
        rows, cols, heads, DH
    )
    d_o = d_go * gate
    delta = jnp.transpose(jnp.sum(d_o * attended, axis=-1), (0, 2, 1))
    grad_out = d_o.astype(jnp.bfloat16)
    d_gate = d_go * attended * gate * (1.0 - gate)
    gathered_back = lax.all_gather(kv_local, "col", axis=1, tiled=True)

    def backward_piece(state, piece):
        length = piece.shape[2]
        step = math.gcd(length, 2 * TILE)

        def backward_one_block(number, inner):
            offset = number * step
            first = offset
            bias_blk, key_blk, value_blk, mask = block_parts(
                gathered_back, piece, offset, first, step
            )

            def backward_update(carry):
                dq_acc, dkv_acc = carry
                score = scores(key_blk, bias_blk, mask)
                prob = jnp.where(mask[None, None], jnp.exp(score - lse[..., None]), 0.0)
                d_value = jnp.einsum(
                    "rhjk,rjhd->rkhd",
                    prob.astype(jnp.bfloat16),
                    grad_out,
                    preferred_element_type=jnp.float32,
                )
                d_prob = jnp.einsum(
                    "rjhd,rkhd->rhjk", grad_out, value_blk, preferred_element_type=jnp.float32
                )
                d_score = (prob * (d_prob - delta[..., None])).astype(jnp.bfloat16)
                dq_acc = dq_acc + jnp.einsum(
                    "rhjk,rkhd->rhjd", d_score, key_blk, preferred_element_type=jnp.float32
                )
                d_key = jnp.einsum(
                    "rhjk,rjhd->rkhd", d_score, query, preferred_element_type=jnp.float32
                )
                both = jnp.stack([d_key, d_value], axis=3).reshape(rows, step, heads * 2 * DH)
                current = lax.dynamic_slice_in_dim(dkv_acc, first, step, 1)
                dkv_acc = lax.dynamic_update_slice_in_dim(dkv_acc, current + both, first, 1)
                return (dq_acc, dkv_acc)

            return lax.cond(jnp.any(mask), backward_update, lambda carry: carry, inner)

        return lax.fori_loop(0, length // step, backward_one_block, state)

    back_state = (
        jnp.zeros((rows, heads, cols, DH), jnp.float32),
        jnp.zeros(gathered_back.shape, jnp.float32),
    )
    dq_acc, dkv_acc = backward_piece(
        back_state, lax.all_gather(tri_bias, "row", axis=2, tiled=True)
    )
    dkv_own = lax.psum_scatter(
        dkv_acc.astype(jnp.bfloat16), "col", scatter_dimension=1, tiled=True
    ).astype(jnp.float32)
    dkv_own = dkv_own.reshape(rows, cols, heads, 2, DH)
    d_query = jnp.transpose(dq_acc, (0, 2, 1, 3)) * scale
    d_proj = jnp.stack([d_query, dkv_own[:, :, :, 0], dkv_own[:, :, :, 1], d_gate], axis=3)
    d_proj = d_proj.astype(jnp.bfloat16).reshape(rows, cols, heads * 4 * DH)
    d_norm = jnp.einsum("rjf,cf->rjc", d_proj, w_proj, preferred_element_type=jnp.float32)
    d_norm = lax.psum(d_norm.astype(jnp.bfloat16), "head").astype(jnp.float32)
    input_gradient = d_norm * layer_norm_gain
    pair_gradient = inverse_deviation * (
        input_gradient
        - jnp.mean(input_gradient, axis=-1, keepdims=True)
        - standardized_input * jnp.mean(input_gradient * standardized_input, axis=-1, keepdims=True)
    )
    pair_gradient = pair_gradient.astype(jnp.bfloat16)
    return (out, pair_gradient)


def solution(mesh):
    in_specs = (
        P("row", "col", None),
        P(),
        P(None, "head"),
        P("head", None),
        P("head", "col", "row"),
        P(),
        P("row", "col", None),
    )
    out_specs = (P("row", "col", "head"), P("row", "col", None))
    return jax.shard_map(
        per_device, mesh=mesh, in_specs=in_specs, out_specs=out_specs, check_vma=False
    )
```

profile of v0, /device:TPU:1, one launch (start us, length us, event | category | flops | bytes accessed | tf_op | source)
XLA Modules:
  0.0 569.7 jit_solution(15667866155526611855)
XLA Ops:
  7.2 1.8 copy.41
  9.1 1.0 convert_reduce_fusion
  10.2 1.1 fusion.36
  11.3 1.3 fusion.38
  13.9 71.6 %all-gather.5.cloned.1.call-done = bf16[2,128,4096]{1,2,0:T(8,128)(2,1)} async-done(((bf16[2,128,512]{1,2,0:T(8,128)(2,1)}), bf16[2,128,4096]{1,2,0:T(8,128)(2,1)}) %all-gather.5.cloned.1.call-update) | async-done | bytes 2097168 | tf_op jit(solution)/shard_map/all_gather | solution.py:58
  85.5 123.1 %all-gather.3.cloned.1.call-done = bf16[4,4096,128]{1,2,0:T(8,128)(2,1)} async-done(((bf16[4,128,128]{1,2,0:T(8,128)(2,1)}), bf16[4,4096,128]{1,2,0:T(8,128)(2,1)}) %all-gather.3.cloned.1.call-update) | async-done | bytes 4194320 | tf_op jit(solution)/shard_map/all_gather | solution.py:38
  208.6 28.2 %while.36 = (s32[]{:T(128)}, f32[4,2,128]{2,1,0:T(2,128)S(1)}, f32[4,2,128]{2,1,0:T(2,128)S(1)}, f32[4,2,128,32]{2,3,1,0:T(8,128)S(1)}, bf16[128,16]{0,1:T(8,128...) while((s32[]{:T(128)}, f32[4,2,128]{2,1,0:T(2,128)S(1)}, ...), condition=%wide.region_8.9_spmd, body=%wide.region_2.8_spmd.sunk | while | flops 76367872 | bytes 10887453 | solution.py:83
  210.1 4.1 conditional.4
  210.1 1.1 constant_dynamic-slice_fusion
  211.2 1.0 dynamic-slice_convert_fusion
  218.6 4.1 conditional.4
  218.6 1.1 constant_dynamic-slice_fusion
  219.7 1.0 dynamic-slice_convert_fusion
  224.2 4.1 conditional.4
  224.2 1.1 constant_dynamic-slice_fusion
  225.3 1.0 dynamic-slice_convert_fusion
  231.2 4.1 conditional.4
  231.2 1.1 constant_dynamic-slice_fusion
  232.3 1.0 dynamic-slice_convert_fusion
  236.9 4.2 broadcast_in_dim.98
  241.2 41.5 %while.37 = (s32[]{:T(128)}, f32[4,2,128,32]{2,3,1,0:T(8,128)S(1)}, f32[4,4096,128]{1,2,0:T(8,128)}, bf16[128,16]{0,1:T(8,128)(2,1)S(1)}, bf16[4,4096,128]{1,2,0...) while((s32[]{:T(128)}, f32[4,2,128,32]{2,3,1,0:T(8,128)S(1)}, ...), condition=%wide.region_15.16_spmd, body=%wide.region_11.15_spmd.sunk | while | flops 174899200 | bytes 21643568 | solution.py:138
  242.7 7.3 %conditional.5 = ((f32[4,2,128,32]{2,3,1,0:T(8,128)S(1)}, f32[4,4096,128]{1,2,0:T(8,128)})) conditional(s32[]{:T(128)} %convert_element_type.174, (f32[4,2,128,32]{2,3,1,0:T(8,128)S(1)}, f32[4,4096,128]{1,2,0:T(8,128)}) %tuple.125, (pred[128,512]{0,1:T(8,128)(4,1)S(1)}, s32[]{:T(128)}, bf16[4,4096,128]{1,2,0:T(8,128)(2,1)}, ...), branch_computations={%region_13.13_spmd, %region_14.14_spmd} | conditional | flops 172654592 | bytes 21569606 | solution.py:136
  242.7 1.1 constant_dynamic-slice_fusion.1
  243.8 1.0 dynamic-slice_convert_fusion.1
  247.6 2.4 constant_dynamic-update-slice_fusion
  254.7 7.3 %conditional.5 = ((f32[4,2,128,32]{2,3,1,0:T(8,128)S(1)}, f32[4,4096,128]{1,2,0:T(8,128)})) conditional(s32[]{:T(128)} %convert_element_type.174, (f32[4,2,128,32]{2,3,1,0:T(8,128)S(1)}, f32[4,4096,128]{1,2,0:T(8,128)}) %tuple.125, (pred[128,512]{0,1:T(8,128)(4,1)S(1)}, s32[]{:T(128)}, bf16[4,4096,128]{1,2,0:T(8,128)(2,1)}, ...), branch_computations={%region_13.13_spmd, %region_14.14_spmd} | conditional | flops 172654592 | bytes 21569606 | solution.py:136
  254.8 1.1 constant_dynamic-slice_fusion.1
  255.8 1.0 dynamic-slice_convert_fusion.1
  259.6 2.4 constant_dynamic-update-slice_fusion
  263.5 7.2 %conditional.5 = ((f32[4,2,128,32]{2,3,1,0:T(8,128)S(1)}, f32[4,4096,128]{1,2,0:T(8,128)})) conditional(s32[]{:T(128)} %convert_element_type.174, (f32[4,2,128,32]{2,3,1,0:T(8,128)S(1)}, f32[4,4096,128]{1,2,0:T(8,128)}) %tuple.125, (pred[128,512]{0,1:T(8,128)(4,1)S(1)}, s32[]{:T(128)}, bf16[4,4096,128]{1,2,0:T(8,128)(2,1)}, ...), branch_computations={%region_13.13_spmd, %region_14.14_spmd} | conditional | flops 172654592 | bytes 21569606 | solution.py:136
  263.6 1.1 constant_dynamic-slice_fusion.1
  264.6 1.0 dynamic-slice_convert_fusion.1
  268.4 2.4 constant_dynamic-update-slice_fusion
  270.8 0.9 fusion.85
  273.9 7.2 %conditional.5 = ((f32[4,2,128,32]{2,3,1,0:T(8,128)S(1)}, f32[4,4096,128]{1,2,0:T(8,128)})) conditional(s32[]{:T(128)} %convert_element_type.174, (f32[4,2,128,32]{2,3,1,0:T(8,128)S(1)}, f32[4,4096,128]{1,2,0:T(8,128)}) %tuple.125, (pred[128,512]{0,1:T(8,128)(4,1)S(1)}, s32[]{:T(128)}, bf16[4,4096,128]{1,2,0:T(8,128)(2,1)}, ...), branch_computations={%region_13.13_spmd, %region_14.14_spmd} | conditional | flops 172654592 | bytes 21569606 | solution.py:136
  273.9 1.1 constant_dynamic-slice_fusion.1
  275.0 1.0 dynamic-slice_convert_fusion.1
  278.8 2.4 constant_dynamic-update-slice_fusion
  282.7 6.0 %convert_element_type.115 = bf16[4,4096,128]{1,2,0:T(8,128)(2,1)} convert(f32[4,4096,128]{1,2,0:T(8,128)} %get-tuple-element.755) | non-fusion elementwise | flops 2097152 | bytes 12582912 | tf_op jit(solution)/shard_map/convert_element_type | solution.py:148
  288.7 7.5 %copy.50 = bf16[4,4096,128]{2,0,1:T(4,128)(2,1)} copy(bf16[4,4096,128]{1,2,0:T(8,128)(2,1)} %convert_element_type.115) | data formatting | bytes 8388608
  296.2 4.9 copy.58
  301.2 183.6 %reduce-scatter.7.cloned.1.call-done = bf16[128,512]{1,0:T(8,128)(2,1)} async-done(((bf16[4096,512]{1,0:T(8,128)(2,1)}), bf16[128,512]{1,0:T(8,128)(2,1)}) %reduce-scatter.7.cloned.1.call-update) | async-done | bytes 131088
  484.8 0.9 reshape.164
  485.9 0.9 convolution_convert_fusion
  487.8 52.9 %all-reduce.2.cloned.1.call-done = bf16[4,128,128]{2,1,0:T(8,128)(2,1)} async-done(((bf16[4,128,128]{2,1,0:T(8,128)(2,1)}), bf16[4,128,128]{2,1,0:T(8,128)(2,1)}) %all-reduce.2.cloned.1.call-update) | async-done | bytes 131088 | tf_op jit(solution)/shard_map/psum | solution.py:155
  540.7 1.3 fusion.37
  542.0 1.9 fusion.35
  543.9 19.3 %reduce-scatter.5.cloned.1.call-done = bf16[4,128,64]{1,2,0:T(8,128)(2,1)} async-done(((bf16[4,128,128]{1,2,0:T(8,128)(2,1)}), bf16[4,128,64]{1,2,0:T(8,128)(2,1)}) %reduce-scatter.5.cloned.1.call-update) | async-done | bytes 65552 | tf_op jit(solution)/shard_map/reduce_scatter | solution.py:88
  (131 shorter events, 34.8 us)
Async XLA Ops:
  7.2 6.5 %copy-start = (bf16[4,128,128]{2,1,0:T(8,128)(2,1)S(1)}, bf16[4,128,128]{2,1,0:T(8,128)(2,1)}, u32[]{:S(2)}) copy-start(bf16[4,128,128]{2,1,0:T(8,128)(2,1)} %param.21) | copy-start | bytes 393220
  7.2 6.3 %copy-start.5 = (s32[16,16]{1,0:T(8,128)S(1)}, s32[16,16]{1,0:T(8,128)}, u32[]{:S(2)}) copy-start(s32[16,16]{1,0:T(8,128)} %param.20) | copy-start | bytes 3076
  7.2 6.5 %copy-start.3 = (bf16[64,128]{1,0:T(8,128)(2,1)S(1)}, bf16[64,128]{1,0:T(8,128)(2,1)}, u32[]{:S(2)}) copy-start(bf16[64,128]{1,0:T(8,128)(2,1)} %param.18) | copy-start | bytes 49156
  7.2 78.3 %all-gather.5.cloned.1.call-start = ((), (), s32[]{:S(2)}) async-start(), calls=%async_computation.3 | async-start | bytes 2359296 | tf_op jit(solution)/shard_map/all_gather | solution.py:58
  9.1 199.5 %all-gather.3.cloned.1.call-start = ((), (), s32[]{:S(2)}) async-start(), calls=%async_computation.2 | async-start | bytes 4325376 | tf_op jit(solution)/shard_map/all_gather | solution.py:38
  13.4 471.4 %reduce-scatter.7.cloned.1.call-start = ((), (), s32[]{:S(2)}) async-start(), calls=%async_computation.6 | async-start | bytes 4325376
  301.0 184.9 %copy-start.2 = (bf16[128,256]{1,0:T(8,128)(2,1)S(1)}, bf16[128,256]{1,0:T(8,128)(2,1)}, u32[]{:S(2)}) copy-start(bf16[128,256]{1,0:T(8,128)(2,1)} %param.17) | copy-start | bytes 196612
  301.1 239.6 %copy-start.1 = (bf16[4,128,128]{2,1,0:T(8,128)(2,1)S(1)}, bf16[4,128,128]{2,1,0:T(8,128)(2,1)}, u32[]{:S(2)}) copy-start(bf16[4,128,128]{2,1,0:T(8,128)(2,1)} %param.15) | copy-start | bytes 393220
  301.1 239.6 %copy-start.4 = (f32[128]{0:T(128)S(1)}, f32[128]{0:T(128)}, u32[]{:S(2)}) copy-start(f32[128]{0:T(128)} %param.16) | copy-start | bytes 1540
  301.1 239.6 %all-reduce.2.cloned.1.call-start = ((), (), s32[]{:S(2)}) async-start(), calls=%async_computation.5 | async-start | bytes 262144 | tf_op jit(solution)/shard_map/psum | solution.py:155
  486.9 76.3 %reduce-scatter.5.cloned.1.call-start = ((), (), s32[]{:S(2)}) async-start(), calls=%async_computation.4 | async-start | bytes 196608 | tf_op jit(solution)/shard_map/reduce_scatter | solution.py:88
Sparse Core Ops, SparseCore 0:
  11.2 74.2 all-gather.4
  88.0 120.4 all-gather.2
  301.2 183.5 reduce-scatter.6
  488.1 52.5 all-reduce.1
  543.9 19.2 reduce-scatter.4
where the time goes:
time: 572 us; the launch traced here: 570 us
  waiting for transfers between devices  451 us (79%)
  matrix products  33.4 us (6%)
  other arithmetic  31.8 us (6%)
  local copies, waits for them, and re-layouts  29.2 us (5%)
  between operations  14 us (2%)
  loops' own time  10.5 us (2%)
    unnamed x6, waiting for transfers between devices  184 us
    all_gather x1, waiting for transfers between devices, per_device(): gathered = lax.all_gather(kv_local, 'col', axis=1, tiled=True)  123 us
    all_gather x1, waiting for transfers between devices, per_device(): piece = lax.all_gather(tri_bias, 'row', axis=2, tiled=True)  71.6 us
    psum x1, waiting for transfers between devices, per_device(): d_norm = lax.psum(d_norm.astype(jnp.bfloat16), 'head').astype(jnp.float32)  52.9 us
    reduce_scatter x1, waiting for transfers between devices, per_device(): lax.psum_scatter(partial_out.astype(jnp.bfloat16), 'head', scatter_dimens...  19.3 us
    unnamed x17, local copies, waits for them, and re-layouts  15.3 us
    dot_general x16, matrix products, block_parts(): mask = jnp.dot(row_active, tile_onehot(first, step, tiles_total).T) > 0.5  14.3 us
  transfers between devices with their start and end apart: 5, of which 5 were waited for; matrix products, arithmetic and copies ran while one was open for 2% of the time, Pallas kernels for 0%

commit v1 on v0

--- a/solution.py
+++ b/solution.py
@@ -152,7 +152,9 @@
     d_proj = jnp.stack([d_query, dkv_own[:, :, :, 0], dkv_own[:, :, :, 1], d_gate], axis=3)
     d_proj = d_proj.astype(jnp.bfloat16).reshape(rows, cols, heads * 4 * DH)
     d_norm = jnp.einsum("rjf,cf->rjc", d_proj, w_proj, preferred_element_type=jnp.float32)
-    d_norm = lax.psum(d_norm.astype(jnp.bfloat16), "head").astype(jnp.float32)
+    d_norm = jnp.sum(lax.all_gather(d_norm.astype(jnp.bfloat16), "head"), axis=0).astype(
+        jnp.float32
+    )
     input_gradient = d_norm * layer_norm_gain
     pair_gradient = inverse_deviation * (
         input_gradient

time: 572 us -> 531 us (0.928)
  waiting for transfers between devices: 451 us -> 386 us
  blocking collectives: 0 us -> 23.2 us
    psum x1 -> x0, waiting for transfers between devices: 52.9 us -> none  [per_device(): d_norm = lax.psum(d_norm.astype(jnp.bfloat16), 'head').astype(jnp.float32)]
    all_gather x0 -> x1, blocking collectives: none -> 23.2 us  [per_device(): lax.all_gather(d_norm.astype(jnp.bfloat16), 'head')]
    reduce_scatter x1, waiting for transfers between devices: 19.3 us -> 8.6 us  [per_device(): lax.psum_scatter(partial_out.astype(jnp.bfloat16), 'head', scatter_dimens...]
    unnamed x6 -> x5, waiting for transfers between devices: 184 us -> 183 us
  transfers between devices with their start and end apart: 5 -> 4, of which waited for: 5 -> 4; matrix products, arithmetic and copies ran while one was open for 2% -> 2% of each run, Pallas kernels for 0% -> 0%
where the time goes in v1:
time: 531 us; the launch traced here: 529 us
  waiting for transfers between devices  386 us (73%)
  matrix products  34 us (6%)
  other arithmetic  30 us (6%)
  local copies, waits for them, and re-layouts  29.2 us (5%)
  blocking collectives  23.2 us (4%)
  between operations  14 us (3%)
  loops' own time  12.2 us (2%)
    unnamed x5, waiting for transfers between devices  183 us
    all_gather x1, waiting for transfers between devices, per_device(): gathered = lax.all_gather(kv_local, 'col', axis=1, tiled=True)  123 us
    all_gather x1, waiting for transfers between devices, per_device(): piece = lax.all_gather(tri_bias, 'row', axis=2, tiled=True)  71.6 us
    all_gather x1, blocking collectives, per_device(): lax.all_gather(d_norm.astype(jnp.bfloat16), 'head')  23.2 us
    dot_general x16, matrix products, block_parts(): mask = jnp.dot(row_active, tile_onehot(first, step, tiles_total).T) > 0.5  15.5 us
    unnamed x17, local copies, waits for them, and re-layouts  15.2 us
  transfers between devices with their start and end apart: 4, of which 4 were waited for; matrix products, arithmetic and copies ran while one was open for 2% of the time, Pallas kernels for 0%

profile of v1, /device:TPU:1, one launch (start us, length us, event | category | flops | bytes accessed | tf_op | source)
XLA Modules:
  0.0 528.9 jit_solution(17225977970667857129)
XLA Ops:
  7.2 1.8 copy.41
  9.1 1.0 convert_reduce_fusion
  10.2 1.1 fusion.36
  11.3 1.3 fusion.38
  13.9 71.6 %all-gather.6.cloned.1.call-done = bf16[2,128,4096]{1,2,0:T(8,128)(2,1)} async-done(((bf16[2,128,512]{1,2,0:T(8,128)(2,1)}), bf16[2,128,4096]{1,2,0:T(8,128)(2,1)}) %all-gather.6.cloned.1.call-update) | async-done | bytes 2097168 | tf_op jit(solution)/shard_map/all_gather | solution.py:58
  85.5 123.1 %all-gather.4.cloned.1.call-done = bf16[4,4096,128]{1,2,0:T(8,128)(2,1)} async-done(((bf16[4,128,128]{1,2,0:T(8,128)(2,1)}), bf16[4,4096,128]{1,2,0:T(8,128)(2,1)}) %all-gather.4.cloned.1.call-update) | async-done | bytes 4194320 | tf_op jit(solution)/shard_map/all_gather | solution.py:38
  208.6 29.9 %while.36 = (s32[]{:T(128)}, f32[4,2,128]{2,1,0:T(2,128)S(1)}, f32[4,2,128]{2,1,0:T(2,128)S(1)}, f32[4,2,128,32]{2,3,1,0:T(8,128)S(1)}, bf16[128,16]{0,1:T(8,128...) while((s32[]{:T(128)}, f32[4,2,128]{2,1,0:T(2,128)S(1)}, ...), condition=%wide.region_8.9_spmd, body=%wide.region_2.8_spmd.sunk | while | flops 76367872 | bytes 10887453 | solution.py:83
  210.3 4.1 conditional.4
  210.3 1.1 constant_dynamic-slice_fusion
  211.4 1.0 dynamic-slice_convert_fusion
  219.5 4.1 conditional.4
  219.5 1.1 constant_dynamic-slice_fusion
  220.6 1.0 dynamic-slice_convert_fusion
  225.3 4.1 conditional.4
  225.3 1.1 constant_dynamic-slice_fusion
  226.4 1.0 dynamic-slice_convert_fusion
  232.7 4.1 conditional.4
  232.8 1.1 constant_dynamic-slice_fusion
  233.8 1.0 dynamic-slice_convert_fusion
  238.7 4.3 broadcast_in_dim.98
  242.9 42.6 %while.37 = (s32[]{:T(128)}, f32[4,2,128,32]{2,3,1,0:T(8,128)S(1)}, f32[4,4096,128]{1,2,0:T(8,128)}, bf16[128,16]{0,1:T(8,128)(2,1)S(1)}, bf16[4,4096,128]{1,2,0...) while((s32[]{:T(128)}, f32[4,2,128,32]{2,3,1,0:T(8,128)S(1)}, ...), condition=%wide.region_15.16_spmd, body=%wide.region_11.15_spmd.sunk | while | flops 174899200 | bytes 21643568 | solution.py:138
  242.9 1.0 fusion.85
  244.6 7.3 %conditional.5 = ((f32[4,2,128,32]{2,3,1,0:T(8,128)S(1)}, f32[4,4096,128]{1,2,0:T(8,128)})) conditional(s32[]{:T(128)} %convert_element_type.176, (f32[4,2,128,32]{2,3,1,0:T(8,128)S(1)}, f32[4,4096,128]{1,2,0:T(8,128)}) %tuple.125, (pred[128,512]{0,1:T(8,128)(4,1)S(1)}, s32[]{:T(128)}, bf16[4,4096,128]{1,2,0:T(8,128)(2,1)}, ...), branch_computations={%region_13.13_spmd, %region_14.14_spmd} | conditional | flops 172654592 | bytes 21569606 | solution.py:136
  244.6 1.1 constant_dynamic-slice_fusion.1
  245.7 1.0 dynamic-slice_convert_fusion.1
  249.5 2.4 constant_dynamic-update-slice_fusion
  251.9 1.0 fusion.85
  257.0 7.2 %conditional.5 = ((f32[4,2,128,32]{2,3,1,0:T(8,128)S(1)}, f32[4,4096,128]{1,2,0:T(8,128)})) conditional(s32[]{:T(128)} %convert_element_type.176, (f32[4,2,128,32]{2,3,1,0:T(8,128)S(1)}, f32[4,4096,128]{1,2,0:T(8,128)}) %tuple.125, (pred[128,512]{0,1:T(8,128)(4,1)S(1)}, s32[]{:T(128)}, bf16[4,4096,128]{1,2,0:T(8,128)(2,1)}, ...), branch_computations={%region_13.13_spmd, %region_14.14_spmd} | conditional | flops 172654592 | bytes 21569606 | solution.py:136
  257.1 1.1 constant_dynamic-slice_fusion.1
  258.1 1.0 dynamic-slice_convert_fusion.1
  261.9 2.4 constant_dynamic-update-slice_fusion
  264.3 1.0 fusion.85
  265.9 7.3 %conditional.5 = ((f32[4,2,128,32]{2,3,1,0:T(8,128)S(1)}, f32[4,4096,128]{1,2,0:T(8,128)})) conditional(s32[]{:T(128)} %convert_element_type.176, (f32[4,2,128,32]{2,3,1,0:T(8,128)S(1)}, f32[4,4096,128]{1,2,0:T(8,128)}) %tuple.125, (pred[128,512]{0,1:T(8,128)(4,1)S(1)}, s32[]{:T(128)}, bf16[4,4096,128]{1,2,0:T(8,128)(2,1)}, ...), branch_computations={%region_13.13_spmd, %region_14.14_spmd} | conditional | flops 172654592 | bytes 21569606 | solution.py:136
  266.0 1.1 constant_dynamic-slice_fusion.1
  267.0 1.0 dynamic-slice_convert_fusion.1
  270.8 2.4 constant_dynamic-update-slice_fusion
  276.6 7.2 %conditional.5 = ((f32[4,2,128,32]{2,3,1,0:T(8,128)S(1)}, f32[4,4096,128]{1,2,0:T(8,128)})) conditional(s32[]{:T(128)} %convert_element_type.176, (f32[4,2,128,32]{2,3,1,0:T(8,128)S(1)}, f32[4,4096,128]{1,2,0:T(8,128)}) %tuple.125, (pred[128,512]{0,1:T(8,128)(4,1)S(1)}, s32[]{:T(128)}, bf16[4,4096,128]{1,2,0:T(8,128)(2,1)}, ...), branch_computations={%region_13.13_spmd, %region_14.14_spmd} | conditional | flops 172654592 | bytes 21569606 | solution.py:136
  276.6 1.1 constant_dynamic-slice_fusion.1
  277.7 1.0 dynamic-slice_convert_fusion.1
  281.5 2.4 constant_dynamic-update-slice_fusion
  283.9 1.0 fusion.85
  285.6 6.0 %convert_element_type.117 = bf16[4,4096,128]{1,2,0:T(8,128)(2,1)} convert(f32[4,4096,128]{1,2,0:T(8,128)} %get-tuple-element.755) | non-fusion elementwise | flops 2097152 | bytes 12582912 | tf_op jit(solution)/shard_map/convert_element_type | solution.py:148
  291.6 7.5 %copy.50 = bf16[4,4096,128]{2,0,1:T(4,128)(2,1)} copy(bf16[4,4096,128]{1,2,0:T(8,128)(2,1)} %convert_element_type.117) | data formatting | bytes 8388608
  299.0 4.8 copy.58
  304.9 182.8 %reduce-scatter.7.cloned.1.call-done = bf16[128,512]{1,0:T(8,128)(2,1)} async-done(((bf16[4096,512]{1,0:T(8,128)(2,1)}), bf16[128,512]{1,0:T(8,128)(2,1)}) %reduce-scatter.7.cloned.1.call-update) | async-done | bytes 131088
  489.1 23.2 %all-gather = bf16[8,128,128]{2,1,0:T(8,128)(2,1)S(1)} all-gather(bf16[4,128,128]{2,1,0:T(8,128)(2,1)S(1)} %convolution_convert_fusion), channel_id=2, replica_groups=mesh['row'=8,'col'=32,'head'=2] {'head'}, dimensions={0}, use_global_device_ids=true | all-gather | bytes 393216 | tf_op jit(solution)/shard_map/all_gather | solution.py:155
  512.7 1.0 fusion.35
  513.7 8.6 %reduce-scatter.5.cloned.1.call-done = bf16[4,128,64]{1,2,0:T(8,128)(2,1)} async-done(((bf16[4,128,128]{1,2,0:T(8,128)(2,1)}), bf16[4,128,64]{1,2,0:T(8,128)(2,1)}) %reduce-scatter.5.cloned.1.call-update) | async-done | bytes 65552 | tf_op jit(solution)/shard_map/reduce_scatter | solution.py:88
  (130 shorter events, 34.7 us)
Async XLA Ops:
  7.2 6.5 %copy-start = (bf16[4,128,128]{2,1,0:T(8,128)(2,1)S(1)}, bf16[4,128,128]{2,1,0:T(8,128)(2,1)}, u32[]{:S(2)}) copy-start(bf16[4,128,128]{2,1,0:T(8,128)(2,1)} %param.21) | copy-start | bytes 393220
  7.2 6.3 %copy-start.5 = (s32[16,16]{1,0:T(8,128)S(1)}, s32[16,16]{1,0:T(8,128)}, u32[]{:S(2)}) copy-start(s32[16,16]{1,0:T(8,128)} %param.20) | copy-start | bytes 3076
  7.2 6.5 %copy-start.3 = (bf16[64,128]{1,0:T(8,128)(2,1)S(1)}, bf16[64,128]{1,0:T(8,128)(2,1)}, u32[]{:S(2)}) copy-start(bf16[64,128]{1,0:T(8,128)(2,1)} %param.18) | copy-start | bytes 49156
  7.2 78.3 %all-gather.6.cloned.1.call-start = ((), (), s32[]{:S(2)}) async-start(), calls=%async_computation.3 | async-start | bytes 2359296 | tf_op jit(solution)/shard_map/all_gather | solution.py:58
  9.1 199.5 %all-gather.4.cloned.1.call-start = ((), (), s32[]{:S(2)}) async-start(), calls=%async_computation.2 | async-start | bytes 4325376 | tf_op jit(solution)/shard_map/all_gather | solution.py:38
  13.4 474.3 %reduce-scatter.7.cloned.1.call-start = ((), (), s32[]{:S(2)}) async-start(), calls=%async_computation.5 | async-start | bytes 4325376
  303.9 185.0 %copy-start.2 = (bf16[128,256]{1,0:T(8,128)(2,1)S(1)}, bf16[128,256]{1,0:T(8,128)(2,1)}, u32[]{:S(2)}) copy-start(bf16[128,256]{1,0:T(8,128)(2,1)} %param.17) | copy-start | bytes 196612
  303.9 208.5 %copy-start.1 = (bf16[4,128,128]{2,1,0:T(8,128)(2,1)S(1)}, bf16[4,128,128]{2,1,0:T(8,128)(2,1)}, u32[]{:S(2)}) copy-start(bf16[4,128,128]{2,1,0:T(8,128)(2,1)} %param.15) | copy-start | bytes 393220
  303.9 208.5 %copy-start.4 = (f32[128]{0:T(128)S(1)}, f32[128]{0:T(128)}, u32[]{:S(2)}) copy-start(f32[128]{0:T(128)} %param.16) | copy-start | bytes 1540
  303.9 218.4 %reduce-scatter.5.cloned.1.call-start = ((), (), s32[]{:S(2)}) async-start(), calls=%async_computation.4 | async-start | bytes 196608 | tf_op jit(solution)/shard_map/reduce_scatter | solution.py:88
Sparse Core Ops, SparseCore 0:
  11.2 74.2 all-gather.5
  88.0 120.4 all-gather.3
  304.0 183.6 reduce-scatter.6
  490.9 31.4 reduce-scatter.4
